TPU v7x, 32 devices: a whole 2x2x4 slice. The times are simulated.
32 devices in a mesh: row: 8 (over y, x, core), col: 4 (over z).
Axes of the slice: x: 2, y: 2, z: 4, core: 2. Of those that a mesh axis runs over, the one named last changes fastest.
Arguments:
- embeddings: bfloat16 [4096, 256], P(('row', 'col')), may hold values from -6 to 6
- cotangent: bfloat16 [4096, 256], P(('row', 'col')), may hold values from -6 to 6
- weight: bfloat16 [256, 256], replicated, may hold values from -0.375 to 0.375
- tiles: bfloat16 [32, 128, 128, 128], P(('row', 'col')), may hold values from -0.078125 to 0.078125
- tile_dst: int32 [32, 128], P(('row', 'col')), may hold values from 0 to 3
- tile_src: int32 [32, 128], P(('row', 'col')), may hold values from 0 to 7
- tile_count: int32 [32], P(('row', 'col')), may hold values from 1 to 128, as said below
Outputs:
- output: bfloat16 [4096, 256], P(('row', 'col'))
- grad_embeddings: bfloat16 [4096, 256], P(('row', 'col'))
- grad_weight: float32 [256, 256], replicated
Inputs may be any that keep to these rules, and one draw needn't show every extreme that they name: `tile_count`: at least one device has exactly 128 live slots.
All inputs are finite; a program needn't handle non-finite values.
Results may differ from a plain program's by a relative error of at most 0.012.
Values may be sent and summed in bfloat16 or wider, within the bound.
A program may use at most 128 MiB of HBM per device.

v0:
```python
import math

import jax
import jax.numpy as jnp
from jax import lax
from jax.sharding import PartitionSpec as P


def shards(embeddings, cotangent, weight, tiles, tile_dst, tile_src, tile_count):
    highest = lax.Precision.HIGHEST
    block_rows = embeddings.shape[0]
    feature_width = embeddings.shape[1]
    row_count = lax.axis_size("row")
    column_count = lax.axis_size("col")
    local_tiles = tiles[0]
    dest_ids = tile_dst[0]
    source_ids = tile_src[0]
    slot_ids = jnp.arange(local_tiles.shape[0], dtype=jnp.int32)
    alive_slots = (slot_ids < tile_count[0]).astype(jnp.float32)
    dest_onehot = (dest_ids[:, None] == jnp.arange(column_count, dtype=jnp.int32)[None, :]).astype(
        jnp.float32
    ) * alive_slots[:, None]
    source_onehot = (source_ids[:, None] == jnp.arange(row_count, dtype=jnp.int32)[None, :]).astype(
        jnp.float32
    ) * alive_slots[:, None]
    gathered = lax.all_gather(embeddings, "row", axis=0, tiled=True).reshape(
        row_count, block_rows, feature_width
    )
    chosen = jnp.take(gathered, source_ids, axis=0)
    products = jnp.einsum("tij,tjd->tid", local_tiles, chosen, preferred_element_type=jnp.float32)
    partial_value = jnp.einsum("tc,tid->cid", dest_onehot, products, precision=highest)
    partial_rounded = partial_value.astype(jnp.bfloat16).reshape(
        column_count * block_rows, feature_width
    )
    summed = lax.psum_scatter(
        partial_rounded.astype(jnp.float32).astype(jnp.bfloat16),
        "col",
        scatter_dimension=0,
        tiled=True,
    ).astype(jnp.float32)
    hidden = summed.astype(jnp.bfloat16)
    output = jnp.dot(hidden, weight, preferred_element_type=jnp.float32).astype(jnp.bfloat16)
    user_count = block_rows * row_count * column_count
    scale_factor = 1.0 / math.sqrt(user_count)
    contract_rows = (((0,), (0,)), ((), ()))
    contract_cols = (((1,), (1,)), ((), ()))
    grad_hidden = lax.dot_general(
        cotangent, weight, contract_cols, preferred_element_type=jnp.float32
    ).astype(jnp.bfloat16)
    grad_group = lax.all_gather(grad_hidden, "col", axis=0, tiled=True)
    weight_term = lax.dot_general(
        summed, cotangent.astype(jnp.float32), contract_rows, precision=highest
    )
    grad_weight = lax.psum(weight_term, ("row", "col")) * scale_factor
    dest_rows = grad_group.reshape(column_count, block_rows, feature_width)
    picked = jnp.take(dest_rows, dest_ids, axis=0)
    back_products = jnp.einsum(
        "tji,tjd->tid", local_tiles, picked, preferred_element_type=jnp.float32
    )
    back_partial = jnp.einsum("tr,tid->rid", source_onehot, back_products, precision=highest)
    back_rounded = lax.optimization_barrier(back_partial.astype(jnp.bfloat16)).astype(jnp.float32)
    back_summed = lax.psum_scatter(
        back_rounded.reshape(row_count * block_rows, feature_width).astype(jnp.bfloat16),
        "row",
        scatter_dimension=0,
        tiled=True,
    )
    return (output, back_summed, grad_weight)


def solution(mesh):
    in_specs = (
        P(("row", "col"), None),
        P(("row", "col"), None),
        P(),
        P(("row", "col"), None, None, None),
        P(("row", "col"), None),
        P(("row", "col"), None),
        P(("row", "col")),
    )
    out_specs = (P(("row", "col"), None), P(("row", "col"), None), P())
    return jax.shard_map(shards, mesh=mesh, in_specs=in_specs, out_specs=out_specs, check_vma=False)
```

profile of v0, /device:TPU:0, one launch (start us, length us, event | category | flops | bytes accessed | tf_op | source)
XLA Modules:
  0.0 260.4 jit_solution(8117860961400061152)
XLA Ops:
  8.0 0.0 copy-start
  8.0 0.0 reduce-scatter.3.cloned.1.call-start
  8.1 0.7 fusion.30
  8.7 0.7 compare_and_fusion.1
  9.4 11.6 %all_gather.6 = bf16[1024,256]{1,0:T(8,128)(2,1)S(1)} all-gather(bf16[128,256]{1,0:T(8,128)(2,1)} %param.7), channel_id=1, replica_groups=mesh['row'=8,'col'=4] {'row'}, dimensions={0}, use_global_device_ids=true | all-gather | bytes 589824 | tf_op jit(solution)/shard_map/all_gather | solution.py:26
  21.0 6.5 %gather_fusion = bf16[128,128,256]{2,1,0:T(8,128)(2,1)} fusion(bf16[8,128,256]{2,1,0:T(8,128)(2,1)S(1)} %bitcast.46, s32[1024]{0:T(1024)S(1)} %pad_clamp_fusion.1), kind=kCustom, calls=%fused_computation | custom fusion | bytes 16777728 | tf_op jit(solution)/shard_map/jit(_take)/gather | solution.py:29
  27.5 13.1 %fusion.6 = f32[128,256,128]{2,1,0:T(8,128)} fusion(bf16[128,128,256]{2,1,0:T(8,128)(2,1)} %gather_fusion, pred[128]{0:T(512)(128)(4,1)S(1)} %compare_and_fusion.1, bf16[1,128,128,128]{3,2,1,0:T(8,128)(2,1)} %param.10), kind=kOutput, calls=%fused_computation.8 | convolution fusion | flops 1077936128 | bytes 29360256 | tf_op jit(solution)/shard_map/tij,tjd->tid/dot_general | solution.py:30
  40.6 0.0 copy-start.3
  40.6 17.7 %copy.12 = f32[128,256,128]{1,0,2:T(8,128)} copy(f32[128,256,128]{2,1,0:T(8,128)} %fusion.6) | data formatting | bytes 33554432 | tf_op jit(solution)/shard_map/tij,tjd->tid/dot_general | solution.py:30
  59.0 0.0 copy-done.3
  59.0 0.0 copy-start.1
  59.0 10.8 %fusion.17 = bf16[4,128,256]{2,0,1:T(4,128)(2,1)S(1)} fusion(f32[128,256,128]{1,0,2:T(8,128)} %copy.12, f32[128]{0:T(128)S(1)} %compare_convert_fusion, s32[128]{0:T(128)S(1)} %bitcast.49), kind=kOutput, calls=%fused_computation.17 | convolution fusion | flops 201458688 | bytes 17040384 | tf_op jit(solution)/shard_map/tc,tid->cid/dot_general | solution.py:31
  69.9 0.7 copy.10
  70.6 0.0 reduce-scatter.3.cloned.1.call-update
  70.6 0.0 all-reduce.2.cloned.1.call-start
  70.7 0.0 copy-done
  70.7 0.0 copy-done.1
  70.7 0.2 convolution_convert_fusion
  70.9 15.5 %all_gather.7 = bf16[512,256]{1,0:T(8,128)(2,1)S(1)} all-gather(bf16[128,256]{1,0:T(8,128)(2,1)S(1)} %convolution_convert_fusion), channel_id=1, replica_groups=mesh['row'=8,'col'=4] {'col'}, dimensions={0}, use_global_device_ids=true | all-gather | bytes 327680 | tf_op jit(solution)/shard_map/all_gather | solution.py:50
  86.4 6.5 %gather_fusion.1 = bf16[128,128,256]{2,1,0:T(8,128)(2,1)} fusion(bf16[4,128,256]{2,1,0:T(8,128)(2,1)S(1)} %bitcast.45, s32[1024]{0:T(1024)S(1)} %pad_clamp_fusion), kind=kCustom, calls=%fused_computation.1 | custom fusion | bytes 16777728 | tf_op jit(solution)/shard_map/jit(_take)/gather | solution.py:56
  92.9 12.8 %fusion.4 = f32[128,256,128]{2,1,0:T(8,128)} fusion(bf16[128,128,256]{2,1,0:T(8,128)(2,1)} %gather_fusion.1, pred[128]{0:T(512)(128)(4,1)S(1)} %compare_and_fusion, bf16[1,128,128,128]{3,2,1,0:T(8,128)(2,1)} %param.10), kind=kOutput, calls=%fused_computation.6 | convolution fusion | flops 1077936128 | bytes 29360256 | tf_op jit(solution)/shard_map/tji,tjd->tid/dot_general | solution.py:57
  105.7 0.0 copy-start.4
  105.7 17.7 %copy.13 = f32[128,256,128]{1,0,2:T(8,128)} copy(f32[128,256,128]{2,1,0:T(8,128)} %fusion.4) | data formatting | bytes 33554432 | tf_op jit(solution)/shard_map/tji,tjd->tid/dot_general | solution.py:57
  123.4 0.0 reduce-scatter.3.cloned.1.call-done
  123.4 1.8 fusion.36
  125.2 0.0 all-reduce.2.cloned.1.call-update
  125.2 0.0 reduce-scatter.5.cloned.1.call-start
  125.2 0.0 copy-done.4
  125.2 0.0 copy-start.2
  125.2 10.8 %fusion.14 = bf16[8,128,256]{2,0,1:T(8,128)(2,1)S(1)} fusion(f32[128,256,128]{1,0,2:T(8,128)} %copy.13, f32[128]{0:T(128)S(1)} %compare_convert_fusion, s32[128]{0:T(128)S(1)} %bitcast.50), kind=kOutput, calls=%fused_computation.16 | convolution fusion | flops 402917376 | bytes 17302528 | tf_op jit(solution)/shard_map/tr,tid->rid/dot_general | solution.py:60
  136.1 0.9 copy.11
  137.0 0.0 reduce-scatter.5.cloned.1.call-update
  137.0 0.0 copy-done.2
  137.0 0.8 convolution_convert_fusion.1
  137.8 113.4 %all-reduce.2.cloned.1.call-done = f32[256,256]{1,0:T(8,128)} async-done(((f32[256,256]{1,0:T(8,128)}), f32[256,256]{1,0:T(8,128)}) %all-reduce.2.cloned.1.call-update) | async-done | bytes 262160 | tf_op jit(solution)/shard_map/psum | solution.py:54
  251.3 1.7 broadcast_multiply_fusion
  252.9 0.0 reduce-scatter.5.cloned.1.call-done
  (5 shorter events, 0.0 us)
Async XLA Ops:
  8.0 62.7 %copy-start = (bf16[256,256]{1,0:T(8,128)(2,1)S(1)}, bf16[256,256]{1,0:T(8,128)(2,1)}, u32[]{:S(2)}) copy-start(bf16[256,256]{1,0:T(8,128)(2,1)} %param.9) | copy-start | bytes 393220
  8.0 115.4 %reduce-scatter.3.cloned.1.call-start = ((), (), s32[]{:S(2)}) async-start(), calls=%async_computation.2 | async-start | bytes 327680 | tf_op jit(solution)/shard_map/reduce_scatter | solution.py:35
  40.6 18.4 %copy-start.3 = (s32[1,128]{1,0:T(1,128)S(1)}, s32[1,128]{1,0:T(1,128)}, u32[]{:S(2)}) copy-start(s32[1,128]{1,0:T(1,128)} %param.11) | copy-start | bytes 1540
  59.0 11.7 %copy-start.1 = (bf16[128,256]{1,0:T(8,128)(2,1)S(1)}, bf16[128,256]{1,0:T(8,128)(2,1)}, u32[]{:S(2)}) copy-start(bf16[128,256]{1,0:T(8,128)(2,1)} %param.8) | copy-start | bytes 196612
  70.6 180.6 %all-reduce.2.cloned.1.call-start = ((), (), s32[]{:S(2)}) async-start(), calls=%async_computation.4 | async-start | bytes 524288 | tf_op jit(solution)/shard_map/psum | solution.py:54
  105.7 19.5 %copy-start.4 = (s32[1,128]{1,0:T(1,128)S(1)}, s32[1,128]{1,0:T(1,128)}, u32[]{:S(2)}) copy-start(s32[1,128]{1,0:T(1,128)} %param.12) | copy-start | bytes 1540
  125.2 127.8 %reduce-scatter.5.cloned.1.call-start = ((), (), s32[]{:S(2)}) async-start(), calls=%async_computation.3 | async-start | bytes 589824 | tf_op jit(solution)/shard_map/reduce_scatter | solution.py:62
  125.2 11.8 %copy-start.2 = (bf16[128,256]{1,0:T(8,128)(2,1)S(1)}, bf16[128,256]{1,0:T(8,128)(2,1)}, u32[]{:S(2)}) copy-start(bf16[128,256]{1,0:T(8,128)(2,1)} %reduce-scatter.3.cloned.1.call-done) | copy-start | bytes 196612
Sparse Core Ops, SparseCore 0:
  70.7 20.6 reduce-scatter.2
  125.3 125.9 all-reduce.1
Sparse Core Ops, SparseCore 1:
  137.1 34.8 reduce-scatter.4
where the time goes:
time: 261 us; the launch traced here: 260 us
  waiting for transfers between devices  113 us (43%)
  matrix products  50.3 us (19%)
  local copies, waits for them, and re-layouts  50 us (19%)
  blocking collectives  27.1 us (10%)
  between operations  16.3 us (6%)
  other arithmetic  3.05 us (1%)
    psum x1, waiting for transfers between devices, shards(): grad_weight = lax.psum(weight_term, ('row', 'col')) * scale_factor  113 us
    dot_general x1, local copies, waits for them, and re-layouts, shards(): jnp.einsum('tij,tjd->tid', local_tiles, chosen, preferred_element_type=jn...  17.7 us
    dot_general x1, local copies, waits for them, and re-layouts, shards(): jnp.einsum('tji,tjd->tid', local_tiles, picked, preferred_element_type=jn...  17.7 us
    all_gather x1, blocking collectives, shards(): grad_group = lax.all_gather(grad_hidden, 'col', axis=0, tiled=True)  15.5 us
    dot_general x1, matrix products, shards(): jnp.einsum('tij,tjd->tid', local_tiles, chosen, preferred_element_type=jn...  13.1 us
    dot_general x1, matrix products, shards(): jnp.einsum('tji,tjd->tid', local_tiles, picked, preferred_element_type=jn...  12.8 us
    all_gather x1, blocking collectives, shards(): lax.all_gather(embeddings, 'row', axis=0, tiled=True)  11.6 us
    dot_general x1, matrix products, shards(): jnp.einsum('tc,tid->cid', dest_onehot, products, precision=highest)  10.8 us
  transfers between devices with their start and end apart: 3, of which 1 were waited for; matrix products, arithmetic and copies ran while one was open for 20% of the time, Pallas kernels for 0%

commit v1 on v0

v1 whole, which is shorter than its diff:
```python
import functools
import math

import jax
import jax.numpy as jnp
from jax import lax
from jax.experimental import pallas as pl
from jax.experimental.pallas import tpu as pltpu
from jax.sharding import PartitionSpec as P

F32 = jnp.float32
BF16 = jnp.bfloat16
ROWS_ROWS = (((0,), (0,)), ((), ()))
COLS_COLS = (((1,), (1,)), ((), ()))
CHUNKS = 4


def fused(
    n_row,
    n_col,
    link_ref,
    emb_ref,
    cot_ref,
    weight_ref,
    tiles_ref,
    out_ref,
    gemb_ref,
    gw_ref,
    tbuf,
    chain,
    a_rows,
    a_cols,
    e_all,
    c_all,
    part,
    part_in,
    back_sib,
    back_sib_in,
    back_own,
    back_sum,
    back_in,
    term,
    term_in,
    mid_in,
    fin,
    tile_sem,
    e_send,
    e_recv,
    relay_send,
    c_send,
    c_recv,
    p_send,
    p_recv,
    s_send,
    s_recv,
    b_send,
    b_recv,
    t_send,
    t_recv,
    m_send,
    m_recv,
    f_send,
    f_recv,
):
    block, width = emb_ref.shape
    slots = tiles_ref.shape[0]
    n_chip = n_row // 2
    row = lax.axis_index("row")
    col = lax.axis_index("col")
    core = lax.rem(row, 2)
    chip = row // 2
    sibling = row + 1 - 2 * core
    row_peers = [lax.rem(row + i, n_row) for i in range(1, n_row)]
    col_peers = [lax.rem(col + i, n_col) for i in range(1, n_col)]
    chip_peers = [lax.rem(chip + i, n_chip) for i in range(1, n_chip)]

    def remote(src, dst, send, recv, r, c):
        return pltpu.make_async_remote_copy(
            src_ref=src,
            dst_ref=dst,
            send_sem=send,
            recv_sem=recv,
            device_id=(r, c),
            device_id_type=pl.DeviceIdType.MESH,
        )

    sent = []

    def send(*args):
        copy = remote(*args)
        copy.start()
        sent.append(copy)

    def arrived(dst, sems, index):
        remote(dst.at[index], dst.at[index], sems.at[index], sems.at[index], sibling, col).wait_recv()

    per = slots // CHUNKS
    loads = []
    for i in range(CHUNKS):
        span = pl.ds(i * per, per)
        load = pltpu.make_async_copy(tiles_ref.at[span], tbuf.at[span], tile_sem.at[i])
        load.start()
        loads.append(load)

    barrier = pltpu.get_barrier_semaphore()
    for r in row_peers:
        pl.semaphore_signal(barrier, inc=1, device_id=(r, col), device_id_type=pl.DeviceIdType.MESH)
    for c in col_peers:
        pl.semaphore_signal(barrier, inc=1, device_id=(row, c), device_id_type=pl.DeviceIdType.MESH)
    pl.semaphore_wait(barrier, n_row + n_col - 2)

    for p in chip_peers:
        r = 2 * p + core
        send(emb_ref, e_all.at[row], e_send.at[r], e_recv.at[row], r, col)
    for c in col_peers:
        send(cot_ref, c_all.at[col], c_send.at[c], c_recv.at[col], row, c)
    send(emb_ref, e_all.at[row], e_send.at[sibling], e_recv.at[row], sibling, col)

    e_all[row] = emb_ref[...]
    c_all[col] = cot_ref[...]

    def relay(p):
        r = 2 * p + core
        arrived(e_all, e_recv, r)
        send(e_all.at[r], e_all.at[r], relay_send.at[r], e_recv.at[r], sibling, col)

    chain[0] = jnp.zeros((block, block), F32)

    def add_tile(t, carry):
        chain[t + 1] = tbuf[t].astype(F32) + chain[link_ref[t]]
        return carry

    waiting = list(chip_peers)
    for i in range(CHUNKS):
        loads[i].wait()
        lax.fori_loop(i * per, (i + 1) * per, add_tile, 0)
        if i > 0 and waiting:
            relay(waiting.pop(0))
    for p in waiting:
        relay(p)

    for k in range(n_col):
        for j in range(n_row):
            tile = chain[link_ref[slots + k * n_row + j]].astype(BF16)
            a_rows[k, :, pl.ds(j * block, block)] = tile
            a_cols[j, pl.ds(k * block, block), :] = tile

    arrived(e_all, e_recv, sibling)
    for p in chip_peers:
        arrived(e_all, e_recv, 2 * p + 1 - core)

    sources = e_all[...].reshape(n_row * block, width)
    for k in col_peers + [col]:
        part[k] = jnp.dot(a_rows[k], sources, preferred_element_type=F32).astype(BF16)
        if k is not col:
            send(part.at[k], part_in.at[col], p_send.at[k], p_recv.at[col], row, k)

    for c in col_peers:
        arrived(c_all, c_recv, c)
    cot_group = c_all[...].reshape(n_col * block, width)
    own_term = lax.dot_general(
        part[...].reshape(n_col * block, width), cot_group, ROWS_ROWS, preferred_element_type=F32
    )
    term[...] = own_term.astype(BF16).reshape(term.shape)
    for r in row_peers:
        send(term.at[r], term_in.at[row], t_send.at[r], t_recv.at[row], r, col)

    grad_hidden = lax.dot_general(
        cot_group, weight_ref[...], COLS_COLS, preferred_element_type=F32
    ).astype(BF16)

    def back(j):
        return lax.dot_general(a_cols[j], grad_hidden, ROWS_ROWS, preferred_element_type=F32)

    for p in chip_peers + [chip]:
        back_sib[p] = back(2 * p + 1 - core).astype(BF16)
        send(back_sib.at[p], back_sib_in.at[p], s_send.at[p], s_recv.at[p], sibling, col)
    for p in chip_peers + [chip]:
        back_own[p] = back(2 * p + core)

    for p in chip_peers:
        arrived(back_sib_in, s_recv, p)
        back_sum[p] = (back_own[p] + back_sib_in[p].astype(F32)).astype(BF16)
        send(back_sum.at[p], back_in.at[chip], b_send.at[p], b_recv.at[chip], 2 * p + core, col)

    row_sum = term[row].astype(F32)
    for r in row_peers:
        arrived(term_in, t_recv, r)
        row_sum = row_sum + term_in[r].astype(F32)
    mid_in[col] = row_sum.astype(BF16)
    for c in col_peers:
        send(mid_in.at[col], mid_in.at[col], m_send.at[c], m_recv.at[col], row, c)

    total = part[col].astype(F32)
    for c in col_peers:
        arrived(part_in, p_recv, c)
        total = total + part_in[c].astype(F32)
    out_ref[...] = jnp.dot(
        total.astype(BF16), weight_ref[...], preferred_element_type=F32
    ).astype(BF16)

    for c in col_peers:
        arrived(mid_in, m_recv, c)
    whole = mid_in[0].astype(F32)
    for c in range(1, n_col):
        whole = whole + mid_in[c].astype(F32)
    fin[row] = whole.astype(BF16)
    for r in row_peers:
        send(fin.at[row], fin.at[row], f_send.at[r], f_recv.at[row], r, col)

    arrived(back_sib_in, s_recv, chip)
    grad = back_own[chip] + back_sib_in[chip].astype(F32)
    for p in chip_peers:
        arrived(back_in, b_recv, p)
        grad = grad + back_in[p].astype(F32)
    gemb_ref[...] = grad.astype(BF16)

    for r in row_peers:
        arrived(fin, f_recv, r)
    scale = 1.0 / math.sqrt(block * n_row * n_col)
    gw_ref[...] = fin[...].reshape(gw_ref.shape).astype(F32) * scale

    for copy in sent:
        copy.wait_send()


def combined(n_row, n_col, embeddings, cotangent, weight, tiles, tile_dst, tile_src, tile_count):
    block, width = embeddings.shape
    slots = tiles.shape[1]
    pairs = n_row * n_col
    n_chip = n_row // 2
    strip = weight.shape[0] // n_row
    place = jnp.arange(slots, dtype=jnp.int32)
    code = jnp.where(place < tile_count[0], tile_dst[0] * n_row + tile_src[0], -1)
    asked = jnp.concatenate([code, jnp.arange(pairs, dtype=jnp.int32)])
    limit = jnp.minimum(jnp.arange(slots + pairs, dtype=jnp.int32), slots)
    same = (code[None, :] == asked[:, None]) & (place[None, :] < limit[:, None])
    link = jnp.max(jnp.where(same, place[None, :] + 1, 0), axis=1)

    vmem = pl.BlockSpec(memory_space=pltpu.VMEM)
    dma = pltpu.SemaphoreType.DMA
    return pl.pallas_call(
        functools.partial(fused, n_row, n_col),
        out_shape=(
            jax.ShapeDtypeStruct((block, width), BF16),
            jax.ShapeDtypeStruct((block, width), BF16),
            jax.ShapeDtypeStruct(weight.shape, F32),
        ),
        in_specs=[
            pl.BlockSpec(memory_space=pltpu.SMEM),
            vmem,
            vmem,
            vmem,
            pl.BlockSpec(memory_space=pl.ANY),
        ],
        out_specs=(vmem, vmem, vmem),
        scratch_shapes=[
            pltpu.VMEM((slots, block, block), BF16),
            pltpu.VMEM((slots + 1, block, block), F32),
            pltpu.VMEM((n_col, block, n_row * block), BF16),
            pltpu.VMEM((n_row, n_col * block, block), BF16),
            pltpu.VMEM((n_row, block, width), BF16),
            pltpu.VMEM((n_col, block, width), BF16),
            pltpu.VMEM((n_col, block, width), BF16),
            pltpu.VMEM((n_col, block, width), BF16),
            pltpu.VMEM((n_chip, block, width), BF16),
            pltpu.VMEM((n_chip, block, width), BF16),
            pltpu.VMEM((n_chip, block, width), F32),
            pltpu.VMEM((n_chip, block, width), BF16),
            pltpu.VMEM((n_chip, block, width), BF16),
            pltpu.VMEM((n_row, strip, width), BF16),
            pltpu.VMEM((n_row, strip, width), BF16),
            pltpu.VMEM((n_col, strip, width), BF16),
            pltpu.VMEM((n_row, strip, width), BF16),
            dma((CHUNKS,)),
            dma((n_row,)),
            dma((n_row,)),
            dma((n_row,)),
            dma((n_col,)),
            dma((n_col,)),
            dma((n_col,)),
            dma((n_col,)),
            dma((n_chip,)),
            dma((n_chip,)),
            dma((n_chip,)),
            dma((n_chip,)),
            dma((n_row,)),
            dma((n_row,)),
            dma((n_col,)),
            dma((n_col,)),
            dma((n_row,)),
            dma((n_row,)),
        ],
        compiler_params=pltpu.CompilerParams(
            collective_id=0, has_side_effects=True, vmem_limit_bytes=40 * 1024 * 1024
        ),
    )(link, embeddings, cotangent, weight, tiles[0])


def slotwise(n_row, n_col, embeddings, cotangent, weight, tiles, tile_dst, tile_src, tile_count):
    block, width = embeddings.shape
    gathered = lax.all_gather(embeddings, "row", axis=0)
    grad_hidden = lax.dot_general(
        cotangent, weight, COLS_COLS, preferred_element_type=F32
    ).astype(BF16)
    grad_group = lax.all_gather(grad_hidden, "col", axis=0)

    def add_slot(t, sums):
        forward, backward = sums
        k, j = tile_dst[0, t], tile_src[0, t]
        tile = lax.dynamic_index_in_dim(tiles[0], t, 0, keepdims=False)
        source = lax.dynamic_index_in_dim(gathered, j, 0, keepdims=False)
        grad = lax.dynamic_index_in_dim(grad_group, k, 0, keepdims=False)
        ahead = jnp.dot(tile, source, preferred_element_type=F32)
        behind = lax.dot_general(tile, grad, ROWS_ROWS, preferred_element_type=F32)
        ahead = ahead + lax.dynamic_index_in_dim(forward, k, 0, keepdims=False)
        behind = behind + lax.dynamic_index_in_dim(backward, j, 0, keepdims=False)
        return (
            lax.dynamic_update_index_in_dim(forward, ahead, k, 0),
            lax.dynamic_update_index_in_dim(backward, behind, j, 0),
        )

    zeros = (jnp.zeros((n_col, block, width), F32), jnp.zeros((n_row, block, width), F32))
    forward, backward = lax.fori_loop(0, tile_count[0], add_slot, zeros)
    summed = lax.psum_scatter(
        forward.astype(BF16).reshape(n_col * block, width), "col", scatter_dimension=0, tiled=True
    ).astype(F32)
    output = jnp.dot(summed.astype(BF16), weight, preferred_element_type=F32).astype(BF16)
    term = lax.dot_general(
        summed, cotangent.astype(F32), ROWS_ROWS, precision=lax.Precision.HIGHEST
    )
    grad_weight = lax.psum(term, ("row", "col")) * (1.0 / math.sqrt(block * n_row * n_col))
    grad_embeddings = lax.psum_scatter(
        backward.astype(BF16).reshape(n_row * block, width), "row", scatter_dimension=0, tiled=True
    )
    return (output, grad_embeddings, grad_weight)


def solution(mesh):
    n_row, n_col = mesh.shape["row"], mesh.shape["col"]

    def local(embeddings, cotangent, weight, tiles, tile_dst, tile_src, tile_count):
        fits = n_row * n_col <= tiles.shape[1] and n_row % 2 == 0
        fits = fits and tiles.shape[1] % CHUNKS == 0 and weight.shape[0] % (16 * n_row) == 0
        body = functools.partial(combined if fits else slotwise, n_row, n_col)
        return body(embeddings, cotangent, weight, tiles, tile_dst, tile_src, tile_count)

    in_specs = (
        P(("row", "col"), None),
        P(("row", "col"), None),
        P(),
        P(("row", "col"), None, None, None),
        P(("row", "col"), None),
        P(("row", "col"), None),
        P(("row", "col")),
    )
    out_specs = (P(("row", "col"), None), P(("row", "col"), None), P())
    return jax.shard_map(local, mesh=mesh, in_specs=in_specs, out_specs=out_specs, check_vma=False)
```

time: 261 us -> 36.6 us (0.14)
  waiting for transfers between devices: 113 us -> 0 us
  matrix products: 50.3 us -> 0 us
  local copies, waits for them, and re-layouts: 50 us -> 6.73 us
  blocking collectives: 27.1 us -> 0 us
  Pallas kernels: 0 us -> 26.7 us
  between operations: 16.3 us -> 1.31 us
    psum x1 -> x0, waiting for transfers between devices: 113 us -> none  [shards(): grad_weight = lax.psum(weight_term, ('row', 'col')) * scale_factor]
    dot_general x7 -> x0, matrix products: 50.3 us -> none  [the longest x1 13.1 us: shards(): jnp.einsum('tij,tjd->tid', local_tiles, chosen, preferred_element_type=jn...]
    dot_general x2 -> x0, local copies, waits for them, and re-layouts: 35.4 us -> none  [the longest x1 17.7 us: shards(): jnp.einsum('tij,tjd->tid', local_tiles, chosen, preferred_element_type=jn...]
    all_gather x2 -> x0, blocking collectives: 27.1 us -> none  [the longest x1 15.5 us: shards(): grad_group = lax.all_gather(grad_hidden, 'col', axis=0, tiled=True)]
    pallas_call x0 -> x1, Pallas kernels: none -> 26.7 us  [combined(): pl.pallas_call(functools.partial(fused, n_row, n_col), out_shape=(jax.Sha...]
    gather x2 -> x0, local copies, waits for them, and re-layouts: 13 us -> none  [the longest x1 6.54 us: shards(): chosen = jnp.take(gathered, source_ids, axis=0)]
    unnamed x10 -> x11, local copies, waits for them, and re-layouts: 0.03 us -> 6.73 us
  transfers between devices with their start and end apart: 3 -> 0, of which waited for: 1 -> 0; matrix products, arithmetic and copies ran while one was open for 20% -> 0% of each run, Pallas kernels for 0% -> 0%
where the time goes in v1:
time: 36.6 us; the launch traced here: 36.3 us
  Pallas kernels  26.7 us (73%)
  local copies, waits for them, and re-layouts  6.73 us (18%)
  other arithmetic  1.56 us (4%)
  between operations  1.31 us (4%)
    pallas_call x1, Pallas kernels, combined(): pl.pallas_call(functools.partial(fused, n_row, n_col), out_shape=(jax.Sha...  26.7 us
    unnamed x11, local copies, waits for them, and re-layouts  6.73 us

profile of v1, /device:TPU:0, one launch (start us, length us, event | category | flops | bytes accessed | tf_op | source)
XLA Modules:
  0.0 36.3 jit_solution(1548747099709616466)
XLA Ops:
  1.3 0.7 %compare_select_fusion = s32[128]{0:T(128)S(1)} fusion(s32[]{:T(128)} %bitcast.7, s32[1,128]{1,0:T(1,128)} %param.12, s32[1,128]{1,0:T(1,128)} %param.11), kind=kLoop, calls=%fused_computation.3 | loop fusion | flops 512 | bytes 1540 | tf_op jit(solution)/shard_map/jit(_where)/select_n | solution.py:234
  2.0 0.7 %fusion.1 = s32[128]{0:T(128)S(1)} fusion(s32[]{:T(128)} %bitcast.6, s32[1,128]{1,0:T(1,128)} %param.12, s32[1,128]{1,0:T(1,128)} %param.11), kind=kLoop, calls=%fused_computation.7 | loop fusion | flops 512 | bytes 1540 | tf_op jit(solution)/shard_map/eq | solution.py:237
  2.7 0.2 select_reduce_fusion.link_ref
  2.8 0.0 copy-start
  2.9 2.2 %copy-done = bf16[1,128,128,128]{3,2,1,0:T(8,128)(2,1)S(1)} copy-done((bf16[1,128,128,128]{3,2,1,0:T(8,128)(2,1)S(1)}, bf16[1,128,128,128]{3,2,1,0:T(8,128)(2,1)}, u32[]{:S(2)}) %copy-start) | copy-done | bytes 4194328
  5.0 0.0 copy-start.1
  5.0 0.9 %copy-done.1 = bf16[256,256]{1,0:T(8,128)(2,1)S(1)} copy-done((bf16[256,256]{1,0:T(8,128)(2,1)S(1)}, bf16[256,256]{1,0:T(8,128)(2,1)}, u32[]{:S(2)}) %copy-start.1) | copy-done | bytes 131096
  5.9 0.0 copy-start.2
  5.9 0.8 %copy-done.2 = bf16[128,256]{1,0:T(8,128)(2,1)S(1)} copy-done((bf16[128,256]{1,0:T(8,128)(2,1)S(1)}, bf16[128,256]{1,0:T(8,128)(2,1)}, u32[]{:S(2)}) %copy-start.2) | copy-done | bytes 65560
  6.8 0.0 copy-start.3
  6.8 0.8 %copy-done.3 = bf16[128,256]{1,0:T(8,128)(2,1)S(1)} copy-done((bf16[128,256]{1,0:T(8,128)(2,1)S(1)}, bf16[128,256]{1,0:T(8,128)(2,1)}, u32[]{:S(2)}) %copy-start.3) | copy-done | bytes 65560
  7.6 26.7 %shard_map.94 = (bf16[128,256]{1,0:T(8,128)(2,1)S(1)}, bf16[128,256]{1,0:T(8,128)(2,1)S(1)}, f32[256,256]{1,0:T(8,128)S(1)}) custom-call(s32[160]{0:T(256)S(1)} %select_reduce_fusion.link_ref, bf16[128,256]{1,0:T(8,128)(2,1)S(1)} %copy-done.2, bf16[128,256]{1,0:T(8,128)(2,1)S(1)} %copy-done.3, bf16[256,256]{1,0:T(8,128)(2,1)S(1)} %copy-done.1, ...), custom_call_target="tpu_custom_call" | custom-call | tf_op jit(solution)/shard_map/pallas_call | solution.py:242
  34.3 0.6 %copy.14 = bf16[128,256]{1,0:T(8,128)(2,1)} copy(bf16[128,256]{1,0:T(8,128)(2,1)S(1)} %get-tuple-element.8) | data formatting | bytes 131072
  34.9 0.6 %copy.15 = bf16[128,256]{1,0:T(8,128)(2,1)} copy(bf16[128,256]{1,0:T(8,128)(2,1)S(1)} %get-tuple-element.9) | data formatting | bytes 131072
  35.6 0.7 %copy.16 = f32[256,256]{1,0:T(8,128)} copy(f32[256,256]{1,0:T(8,128)S(1)} %get-tuple-element.10) | data formatting | bytes 524288
  (3 shorter events, 0.0 us)
Async XLA Ops:
  2.8 2.2 %copy-start = (bf16[1,128,128,128]{3,2,1,0:T(8,128)(2,1)S(1)}, bf16[1,128,128,128]{3,2,1,0:T(8,128)(2,1)}, u32[]{:S(2)}) copy-start(bf16[1,128,128,128]{3,2,1,0:T(8,128)(2,1)} %param.10) | copy-start | bytes 12582916
  5.0 0.9 %copy-start.1 = (bf16[256,256]{1,0:T(8,128)(2,1)S(1)}, bf16[256,256]{1,0:T(8,128)(2,1)}, u32[]{:S(2)}) copy-start(bf16[256,256]{1,0:T(8,128)(2,1)} %weight_ref.1) | copy-start | bytes 393220
  5.9 0.8 %copy-start.2 = (bf16[128,256]{1,0:T(8,128)(2,1)S(1)}, bf16[128,256]{1,0:T(8,128)(2,1)}, u32[]{:S(2)}) copy-start(bf16[128,256]{1,0:T(8,128)(2,1)} %emb_ref.1) | copy-start | bytes 196612
  6.8 0.8 %copy-start.3 = (bf16[128,256]{1,0:T(8,128)(2,1)S(1)}, bf16[128,256]{1,0:T(8,128)(2,1)}, u32[]{:S(2)}) copy-start(bf16[128,256]{1,0:T(8,128)(2,1)} %cot_ref.1) | copy-start | bytes 196612

commit v2 on v1

--- a/solution.py
+++ b/solution.py
@@ -18,7 +18,9 @@
 def fused(
     n_row,
     n_col,
-    link_ref,
+    count_ref,
+    dst_ref,
+    src_ref,
     emb_ref,
     cot_ref,
     weight_ref,
@@ -26,6 +28,9 @@
     out_ref,
     gemb_ref,
     gw_ref,
+    link_v,
+    link_ref,
+    wbuf,
     tbuf,
     chain,
     a_rows,
@@ -43,6 +48,8 @@
     term_in,
     mid_in,
     fin,
+    link_sem,
+    own_sem,
     tile_sem,
     e_send,
     e_recv,
@@ -94,6 +101,10 @@
     def arrived(dst, sems, index):
         remote(dst.at[index], dst.at[index], sems.at[index], sems.at[index], sibling, col).wait_recv()
 
+    owned = [(emb_ref, e_all.at[row]), (cot_ref, c_all.at[col]), (weight_ref, wbuf)]
+    owned = [pltpu.make_async_copy(a, b, own_sem.at[i]) for i, (a, b) in enumerate(owned)]
+    for copy in owned:
+        copy.start()
     per = slots // CHUNKS
     loads = []
     for i in range(CHUNKS):
@@ -116,24 +127,36 @@
         send(cot_ref, c_all.at[col], c_send.at[c], c_recv.at[col], row, c)
     send(emb_ref, e_all.at[row], e_send.at[sibling], e_recv.at[row], sibling, col)
 
-    e_all[row] = emb_ref[...]
-    c_all[col] = cot_ref[...]
+    for copy in owned:
+        copy.wait()
 
     def relay(p):
         r = 2 * p + core
         arrived(e_all, e_recv, r)
         send(e_all.at[r], e_all.at[r], relay_send.at[r], e_recv.at[r], sibling, col)
 
+    spot = lax.broadcasted_iota(jnp.int32, (1, slots), 1)
+    code = jnp.where(spot < count_ref[0], dst_ref[...] * n_row + src_ref[...], -1)
+    down = jnp.broadcast_to(code, (slots, slots)).T
+    ahead = lax.broadcasted_iota(jnp.int32, (slots, slots), 0)
+    before = (down == code) & (ahead < lax.broadcasted_iota(jnp.int32, (slots, slots), 1))
+    link_v[0:1, :] = jnp.max(jnp.where(before, ahead + 1, 0), axis=0, keepdims=True)
+    ends = down == lax.broadcasted_iota(jnp.int32, (slots, slots), 1)
+    link_v[1:2, :] = jnp.max(jnp.where(ends, ahead + 1, 0), axis=0, keepdims=True)
+    links = pltpu.make_async_copy(link_v, link_ref, link_sem)
+    links.start()
+    links.wait()
+
     chain[0] = jnp.zeros((block, block), F32)
 
     def add_tile(t, carry):
-        chain[t + 1] = tbuf[t].astype(F32) + chain[link_ref[t]]
+        chain[t + 1] = tbuf[t].astype(F32) + chain[link_ref[0, t]]
         return carry
 
     waiting = list(chip_peers)
     for i in range(CHUNKS):
         loads[i].wait()
-        lax.fori_loop(i * per, (i + 1) * per, add_tile, 0)
+        lax.fori_loop(i * per, (i + 1) * per, add_tile, 0, unroll=4)
         if i > 0 and waiting:
             relay(waiting.pop(0))
     for p in waiting:
@@ -141,7 +164,7 @@
 
     for k in range(n_col):
         for j in range(n_row):
-            tile = chain[link_ref[slots + k * n_row + j]].astype(BF16)
+            tile = chain[link_ref[1, k * n_row + j]].astype(BF16)
             a_rows[k, :, pl.ds(j * block, block)] = tile
             a_cols[j, pl.ds(k * block, block), :] = tile
 
@@ -152,8 +175,6 @@
     sources = e_all[...].reshape(n_row * block, width)
     for k in col_peers + [col]:
         part[k] = jnp.dot(a_rows[k], sources, preferred_element_type=F32).astype(BF16)
-        if k is not col:
-            send(part.at[k], part_in.at[col], p_send.at[k], p_recv.at[col], row, k)
 
     for c in col_peers:
         arrived(c_all, c_recv, c)
@@ -166,7 +187,7 @@
         send(term.at[r], term_in.at[row], t_send.at[r], t_recv.at[row], r, col)
 
     grad_hidden = lax.dot_general(
-        cot_group, weight_ref[...], COLS_COLS, preferred_element_type=F32
+        cot_group, wbuf[...], COLS_COLS, preferred_element_type=F32
     ).astype(BF16)
 
     def back(j):
@@ -175,14 +196,6 @@
     for p in chip_peers + [chip]:
         back_sib[p] = back(2 * p + 1 - core).astype(BF16)
         send(back_sib.at[p], back_sib_in.at[p], s_send.at[p], s_recv.at[p], sibling, col)
-    for p in chip_peers + [chip]:
-        back_own[p] = back(2 * p + core)
-
-    for p in chip_peers:
-        arrived(back_sib_in, s_recv, p)
-        back_sum[p] = (back_own[p] + back_sib_in[p].astype(F32)).astype(BF16)
-        send(back_sum.at[p], back_in.at[chip], b_send.at[p], b_recv.at[chip], 2 * p + core, col)
-
     row_sum = term[row].astype(F32)
     for r in row_peers:
         arrived(term_in, t_recv, r)
@@ -191,13 +204,16 @@
     for c in col_peers:
         send(mid_in.at[col], mid_in.at[col], m_send.at[c], m_recv.at[col], row, c)
 
-    total = part[col].astype(F32)
-    for c in col_peers:
-        arrived(part_in, p_recv, c)
-        total = total + part_in[c].astype(F32)
-    out_ref[...] = jnp.dot(
-        total.astype(BF16), weight_ref[...], preferred_element_type=F32
-    ).astype(BF16)
+    for k in col_peers:
+        send(part.at[k], part_in.at[col], p_send.at[k], p_recv.at[col], row, k)
+
+    for p in chip_peers + [chip]:
+        back_own[p] = back(2 * p + core)
+
+    for p in chip_peers:
+        arrived(back_sib_in, s_recv, p)
+        back_sum[p] = (back_own[p] + back_sib_in[p].astype(F32)).astype(BF16)
+        send(back_sum.at[p], back_in.at[chip], b_send.at[p], b_recv.at[chip], 2 * p + core, col)
 
     for c in col_peers:
         arrived(mid_in, m_recv, c)
@@ -208,6 +224,14 @@
     for r in row_peers:
         send(fin.at[row], fin.at[row], f_send.at[r], f_recv.at[row], r, col)
 
+    total = part[col].astype(F32)
+    for c in col_peers:
+        arrived(part_in, p_recv, c)
+        total = total + part_in[c].astype(F32)
+    out_ref[...] = jnp.dot(
+        total.astype(BF16), wbuf[...], preferred_element_type=F32
+    ).astype(BF16)
+
     arrived(back_sib_in, s_recv, chip)
     grad = back_own[chip] + back_sib_in[chip].astype(F32)
     for p in chip_peers:
@@ -224,22 +248,29 @@
         copy.wait_send()
 
 
+def hand_over(*refs):
+    read, write = refs[-2:]
+    reads = [pltpu.make_async_copy(refs[i], refs[i + 6], read.at[i]) for i in range(3)]
+    writes = [pltpu.make_async_copy(refs[i + 6], refs[i + 3], write.at[i]) for i in range(3)]
+    for copy in reads:
+        copy.start()
+    for i in range(3):
+        reads[i].wait()
+        writes[i].start()
+    for copy in writes:
+        copy.wait()
+
+
 def combined(n_row, n_col, embeddings, cotangent, weight, tiles, tile_dst, tile_src, tile_count):
     block, width = embeddings.shape
     slots = tiles.shape[1]
     pairs = n_row * n_col
     n_chip = n_row // 2
     strip = weight.shape[0] // n_row
-    place = jnp.arange(slots, dtype=jnp.int32)
-    code = jnp.where(place < tile_count[0], tile_dst[0] * n_row + tile_src[0], -1)
-    asked = jnp.concatenate([code, jnp.arange(pairs, dtype=jnp.int32)])
-    limit = jnp.minimum(jnp.arange(slots + pairs, dtype=jnp.int32), slots)
-    same = (code[None, :] == asked[:, None]) & (place[None, :] < limit[:, None])
-    link = jnp.max(jnp.where(same, place[None, :] + 1, 0), axis=1)
-
     vmem = pl.BlockSpec(memory_space=pltpu.VMEM)
+    whole = pl.BlockSpec(memory_space=pl.ANY)
     dma = pltpu.SemaphoreType.DMA
-    return pl.pallas_call(
+    results = pl.pallas_call(
         functools.partial(fused, n_row, n_col),
         out_shape=(
             jax.ShapeDtypeStruct((block, width), BF16),
@@ -250,11 +281,16 @@
             pl.BlockSpec(memory_space=pltpu.SMEM),
             vmem,
             vmem,
-            vmem,
-            pl.BlockSpec(memory_space=pl.ANY),
+            whole,
+            whole,
+            whole,
+            whole,
         ],
         out_specs=(vmem, vmem, vmem),
         scratch_shapes=[
+            pltpu.VMEM((2, slots), jnp.int32),
+            pltpu.SMEM((2, slots), jnp.int32),
+            pltpu.VMEM(weight.shape, BF16),
             pltpu.VMEM((slots, block, block), BF16),
             pltpu.VMEM((slots + 1, block, block), F32),
             pltpu.VMEM((n_col, block, n_row * block), BF16),
@@ -272,6 +308,8 @@
             pltpu.VMEM((n_row, strip, width), BF16),
             pltpu.VMEM((n_col, strip, width), BF16),
             pltpu.VMEM((n_row, strip, width), BF16),
+            dma,
+            dma((3,)),
             dma((CHUNKS,)),
             dma((n_row,)),
             dma((n_row,)),
@@ -292,9 +330,16 @@
             dma((n_row,)),
         ],
         compiler_params=pltpu.CompilerParams(
-            collective_id=0, has_side_effects=True, vmem_limit_bytes=40 * 1024 * 1024
+            collective_id=0, has_side_effects=True, vmem_limit_bytes=60 * 1024 * 1024
         ),
-    )(link, embeddings, cotangent, weight, tiles[0])
+    )(tile_count, tile_dst, tile_src, embeddings, cotangent, weight, tiles[0])
+    return pl.pallas_call(
+        hand_over,
+        out_shape=tuple(jax.ShapeDtypeStruct(x.shape, x.dtype) for x in results),
+        in_specs=[whole] * 3,
+        out_specs=(whole,) * 3,
+        scratch_shapes=[pltpu.VMEM(x.shape, x.dtype) for x in results] + [dma((3,)), dma((3,))],
+    )(*results)
 
 
 def slotwise(n_row, n_col, embeddings, cotangent, weight, tiles, tile_dst, tile_src, tile_count):

time: 36.6 us -> 30.3 us (0.83)
  local copies, waits for them, and re-layouts: 6.73 us -> 0 us
  Pallas kernels: 26.7 us -> 28.8 us
  other arithmetic: 1.56 us -> 0 us
    unnamed x11 -> x0, local copies, waits for them, and re-layouts: 6.73 us -> none
    pallas_call x0 -> x1, Pallas kernels: none -> 1.78 us  [combined(): pl.pallas_call(hand_over, out_shape=tuple((jax.ShapeDtypeStruct(x.shape,...]
    select_n x1 -> x0, other arithmetic: 0.68 us -> none  [combined(): jnp.where(place < tile_count[0], tile_dst[0] * n_row + tile_src[0], -1)]
    eq x1 -> x0, other arithmetic: 0.68 us -> none  [combined(): same = (code[None, :] == asked[:, None]) & (place[None, :] < limit[:, None])]
    pallas_call x1, Pallas kernels: 26.7 us -> 27.1 us  [combined(): pl.pallas_call(functools.partial(fused, n_row, n_col), out_shape=(jax.Sha...]
where the time goes in v2:
time: 30.3 us; the launch traced here: 30.1 us
  Pallas kernels  28.8 us (95%)
  between operations  1.29 us (4%)
    pallas_call x1, Pallas kernels, combined(): pl.pallas_call(functools.partial(fused, n_row, n_col), out_shape=(jax.Sha...  27.1 us
    pallas_call x1, Pallas kernels, combined(): pl.pallas_call(hand_over, out_shape=tuple((jax.ShapeDtypeStruct(x.shape,...  1.78 us

profile of v2, /device:TPU:0, one launch (start us, length us, event | category | flops | bytes accessed | tf_op | source)
XLA Modules:
  0.0 30.1 jit_solution(15647957798097999287)
XLA Ops:
  1.3 27.1 %shard_map.94 = (bf16[128,256]{1,0:T(8,128)(2,1)}, bf16[128,256]{1,0:T(8,128)(2,1)}, f32[256,256]{1,0:T(8,128)}) custom-call(s32[1]{0:T(128)S(6)} %copy.10.count_ref, s32[1,128]{1,0:T(1,128)} %dst_ref.1, s32[1,128]{1,0:T(1,128)} %src_ref.1, bf16[128,256]{1,0:T(8,128)(2,1)} %emb_ref.1, bf16[128,256]{1,0:T(8,128)(2,1)} %cot_ref.1, ...), custom_call_target="tpu_custom_call" | custom-call | tf_op jit(solution)/shard_map/pallas_call | solution.py:273
  28.3 1.8 %shard_map.95 = (bf16[128,256]{1,0:T(8,128)(2,1)}, bf16[128,256]{1,0:T(8,128)(2,1)}, f32[256,256]{1,0:T(8,128)}) custom-call(bf16[128,256]{1,0:T(8,128)(2,1)} %get-tuple-element.6.refs_0_, bf16[128,256]{1,0:T(8,128)(2,1)} %get-tuple-element.7.refs_1_, f32[256,256]{1,0:T(8,128)} %get-tuple-element.8.refs_2_), custom_call_target="tpu_custom_call" | custom-call | tf_op jit(solution)/shard_map/pallas_call | solution.py:336

commit v3 on v2

--- a/solution.py
+++ b/solution.py
@@ -153,13 +153,10 @@
         chain[t + 1] = tbuf[t].astype(F32) + chain[link_ref[0, t]]
         return carry
 
-    waiting = list(chip_peers)
     for i in range(CHUNKS):
         loads[i].wait()
         lax.fori_loop(i * per, (i + 1) * per, add_tile, 0, unroll=4)
-        if i > 0 and waiting:
-            relay(waiting.pop(0))
-    for p in waiting:
+    for p in chip_peers:
         relay(p)
 
     for k in range(n_col):
@@ -186,6 +183,9 @@
     for r in row_peers:
         send(term.at[r], term_in.at[row], t_send.at[r], t_recv.at[row], r, col)
 
+    for k in col_peers[:2]:
+        send(part.at[k], part_in.at[col], p_send.at[k], p_recv.at[col], row, k)
+
     grad_hidden = lax.dot_general(
         cot_group, wbuf[...], COLS_COLS, preferred_element_type=F32
     ).astype(BF16)
@@ -204,7 +204,7 @@
     for c in col_peers:
         send(mid_in.at[col], mid_in.at[col], m_send.at[c], m_recv.at[col], row, c)
 
-    for k in col_peers:
+    for k in col_peers[2:]:
         send(part.at[k], part_in.at[col], p_send.at[k], p_recv.at[col], row, k)
 
     for p in chip_peers + [chip]:

time: 30.3 us -> 29.2 us (0.964)
  Pallas kernels: 28.8 us -> 27.8 us
    pallas_call x1, Pallas kernels: 27.1 us -> 26 us  [combined(): pl.pallas_call(functools.partial(fused, n_row, n_col), out_shape=(jax.Sha...]
where the time goes in v3:
time: 29.2 us; the launch traced here: 29.1 us
  Pallas kernels  27.8 us (95%)
  between operations  1.29 us (4%)
    pallas_call x1, Pallas kernels, combined(): pl.pallas_call(functools.partial(fused, n_row, n_col), out_shape=(jax.Sha...  26 us
    pallas_call x1, Pallas kernels, combined(): pl.pallas_call(hand_over, out_shape=tuple((jax.ShapeDtypeStruct(x.shape,...  1.78 us

profile of v3, /device:TPU:0, one launch (start us, length us, event | category | flops | bytes accessed | tf_op | source)
XLA Modules:
  0.0 29.1 jit_solution(388681678162378487)
XLA Ops:
  1.3 26.0 %shard_map.94 = (bf16[128,256]{1,0:T(8,128)(2,1)}, bf16[128,256]{1,0:T(8,128)(2,1)}, f32[256,256]{1,0:T(8,128)}) custom-call(s32[1]{0:T(128)S(6)} %copy.10.count_ref, s32[1,128]{1,0:T(1,128)} %dst_ref.1, s32[1,128]{1,0:T(1,128)} %src_ref.1, bf16[128,256]{1,0:T(8,128)(2,1)} %emb_ref.1, bf16[128,256]{1,0:T(8,128)(2,1)} %cot_ref.1, ...), custom_call_target="tpu_custom_call" | custom-call | tf_op jit(solution)/shard_map/pallas_call | solution.py:273
  27.3 1.8 %shard_map.95 = (bf16[128,256]{1,0:T(8,128)(2,1)}, bf16[128,256]{1,0:T(8,128)(2,1)}, f32[256,256]{1,0:T(8,128)}) custom-call(bf16[128,256]{1,0:T(8,128)(2,1)} %get-tuple-element.6.refs_0_, bf16[128,256]{1,0:T(8,128)(2,1)} %get-tuple-element.7.refs_1_, f32[256,256]{1,0:T(8,128)} %get-tuple-element.8.refs_2_), custom_call_target="tpu_custom_call" | custom-call | tf_op jit(solution)/shard_map/pallas_call | solution.py:336

commit v4 on v3

--- a/solution.py
+++ b/solution.py
@@ -101,6 +101,12 @@
     def arrived(dst, sems, index):
         remote(dst.at[index], dst.at[index], sems.at[index], sems.at[index], sibling, col).wait_recv()
 
+    barrier = pltpu.get_barrier_semaphore()
+    for r in row_peers:
+        pl.semaphore_signal(barrier, inc=1, device_id=(r, col), device_id_type=pl.DeviceIdType.MESH)
+    for c in col_peers:
+        pl.semaphore_signal(barrier, inc=1, device_id=(row, c), device_id_type=pl.DeviceIdType.MESH)
+
     owned = [(emb_ref, e_all.at[row]), (cot_ref, c_all.at[col]), (weight_ref, wbuf)]
     owned = [pltpu.make_async_copy(a, b, own_sem.at[i]) for i, (a, b) in enumerate(owned)]
     for copy in owned:
@@ -113,11 +119,6 @@
         load.start()
         loads.append(load)
 
-    barrier = pltpu.get_barrier_semaphore()
-    for r in row_peers:
-        pl.semaphore_signal(barrier, inc=1, device_id=(r, col), device_id_type=pl.DeviceIdType.MESH)
-    for c in col_peers:
-        pl.semaphore_signal(barrier, inc=1, device_id=(row, c), device_id_type=pl.DeviceIdType.MESH)
     pl.semaphore_wait(barrier, n_row + n_col - 2)
 
     for p in chip_peers:

time: 29.2 us -> 29.2 us (level)
  no operation moved by 1% of the time
where the time goes in v4:
time: 29.2 us; the launch traced here: 29.1 us
  Pallas kernels  27.8 us (95%)
  between operations  1.29 us (4%)
    pallas_call x1, Pallas kernels, combined(): pl.pallas_call(functools.partial(fused, n_row, n_col), out_shape=(jax.Sha...  26 us
    pallas_call x1, Pallas kernels, combined(): pl.pallas_call(hand_over, out_shape=tuple((jax.ShapeDtypeStruct(x.shape,...  1.78 us

profile of v4, /device:TPU:0, one launch (start us, length us, event | category | flops | bytes accessed | tf_op | source)
XLA Modules:
  0.0 29.1 jit_solution(8809400459690139115)
XLA Ops:
  1.3 26.0 %shard_map.94 = (bf16[128,256]{1,0:T(8,128)(2,1)}, bf16[128,256]{1,0:T(8,128)(2,1)}, f32[256,256]{1,0:T(8,128)}) custom-call(s32[1]{0:T(128)S(6)} %copy.10.count_ref, s32[1,128]{1,0:T(1,128)} %dst_ref.1, s32[1,128]{1,0:T(1,128)} %src_ref.1, bf16[128,256]{1,0:T(8,128)(2,1)} %emb_ref.1, bf16[128,256]{1,0:T(8,128)(2,1)} %cot_ref.1, ...), custom_call_target="tpu_custom_call" | custom-call | tf_op jit(solution)/shard_map/pallas_call | solution.py:274
  27.3 1.8 %shard_map.95 = (bf16[128,256]{1,0:T(8,128)(2,1)}, bf16[128,256]{1,0:T(8,128)(2,1)}, f32[256,256]{1,0:T(8,128)}) custom-call(bf16[128,256]{1,0:T(8,128)(2,1)} %get-tuple-element.6.refs_0_, bf16[128,256]{1,0:T(8,128)(2,1)} %get-tuple-element.7.refs_1_, f32[256,256]{1,0:T(8,128)} %get-tuple-element.8.refs_2_), custom_call_target="tpu_custom_call" | custom-call | tf_op jit(solution)/shard_map/pallas_call | solution.py:337
